TPU v7x, 32 devices: a whole 2x2x4 slice. The times are simulated.
32 devices in a mesh: section: 2 (over core), wide: 16 (over z, y, x).
Axes of the slice: x: 2, y: 2, z: 4, core: 2. Of those that a mesh axis runs over, the one named last changes fastest.
Arguments:
- frames: bfloat16 [1024, 48, 1024], P(('section', 'wide')), may hold values from -6 to 6
- qkv_weight: bfloat16 [1024, 3072], replicated, may hold values from -0.1875 to 0.1875
- out_weight: bfloat16 [1024, 1024], replicated, may hold values from -0.1875 to 0.1875
- proj_weight: bfloat16 [1024, 512], replicated, may hold values from -0.1875 to 0.1875
- mlp_weight: bfloat16 [1536, 1024], replicated, may hold values from -0.15625 to 0.15625
- logit_weight: bfloat16 [1024], replicated, may hold values from -0.1875 to 0.1875
- history: bfloat16 [128, 2048, 512], P(('section', 'wide')), may hold values from -6 to 6
- hist_len: int32 [128], P(('section', 'wide')), may hold values from 1 to 2048, as said below
- hist_mask: int32 [128, 2048], P(('section', 'wide')), may hold values 0 or 1
- req_owner: int32 [24576, 1], P(('section', 'wide')), may hold values from 0 to 31; in each aligned block of 768 rows (0 to 767, 768 to 1535, ...) at most 48 rows name the same one
- req_local: int32 [24576], P(('section', 'wide')), may hold values from 0 to 31
- labels: int32 [24576], P(('section', 'wide')), may hold values 0 or 1
Outputs:
- logits: float32 [24576], P(('section', 'wide'))
- grad_proj: float32 [1024, 512], P(('section', 'wide'))
Inputs may be any that keep to these rules, and one draw needn't show every extreme that they name: `hist_len`: some user has 2048 events and some user has 1. `req_owner`: among the 768 requests of one device at most 48 name the same device, and exactly 48 do on some device.
All inputs are finite; a program needn't handle non-finite values. No bound on the sum of `hist_mask` or of `labels` on one device may be relied on, other than what follows from the above.
Results may differ from a plain program's by a relative error of at most 0.01.
Values may be sent and summed in bfloat16 or wider, within the bound.
No kernel may reach another device: no remote copies, remote signals or barrier semaphores. Data moves between devices by JAX's collectives and lax.ppermute only.
A program may use at most 128 MiB of HBM per device.

v0:
```python
import functools
import math

import jax
import jax.numpy as jnp
from jax import lax
from jax.experimental import pallas as pl
from jax.experimental.pallas import tpu as pltpu
from jax.sharding import PartitionSpec as P

HEADS = 16
FRAMES = 3


EPSILON = 1e-06
MIB = 1024 * 1024


def layer_norm(values):
    center = values - jnp.mean(values, axis=-1, keepdims=True)
    spread = jnp.mean(jnp.square(center), axis=-1, keepdims=True)
    return center * lax.rsqrt(spread + EPSILON)


def dot(left, right):
    return jnp.dot(left, right, preferred_element_type=jnp.float32)


def dot_rows(left, right):
    return lax.dot_general(left, right, (((1,), (1,)), ((), ())), preferred_element_type=jnp.float32)


def dot_columns(left, right):
    return lax.dot_general(left, right, (((0,), (0,)), ((), ())), preferred_element_type=jnp.float32)


def split_rows(values):
    high = values.astype(jnp.bfloat16)
    low = (values - high.astype(jnp.float32)).astype(jnp.bfloat16)
    return jnp.concatenate([high, low], axis=0)


def dot_split(values, right):
    both = dot(split_rows(values), right)
    rows = values.shape[0]
    return both[:rows] + both[rows:]


def encode_kernel(
    tokens,
    frames_ref,
    qkv_hbm,
    out_hbm,
    proj_hbm,
    pooled_ref,
    embedded_ref,
    qkv_ref,
    out_ref,
    proj_ref,
    sems,
    normed_ref,
    scores_ref,
    mixed_rows_ref,
    sums_ref,
):
    group = pl.program_id(0)
    rows, width = normed_ref.shape
    head_dim = width // HEADS
    patches = tokens // FRAMES
    cands = rows // tokens
    lanes = 2 * head_dim
    parts = 3
    copies = [
        pltpu.make_async_copy(
            qkv_hbm.at[:, pl.ds(part * width, width)],
            qkv_ref.at[:, pl.ds(part * width, width)],
            sems.at[part],
        )
        for part in range(parts)
    ]
    copies.append(pltpu.make_async_copy(out_hbm, out_ref, sems.at[parts]))
    copies.append(pltpu.make_async_copy(proj_hbm, proj_ref, sems.at[parts + 1]))

    @pl.when(group == 0)
    def _():
        for copy in copies:
            copy.start()

    inputs = frames_ref[...].astype(jnp.float32)
    sums_ref[pl.ds(pl.multiple_of(group * cands, cands), cands), :] = jnp.sum(
        inputs.reshape(cands, tokens, width), axis=1
    )
    normed_ref[...] = layer_norm(inputs).astype(jnp.bfloat16)

    @pl.when(group == 0)
    def _():
        copies[0].wait()
        copies[1].wait()

    exponent = math.log2(math.e) / math.sqrt(head_dim)
    blocks = rows // lanes
    pairs = HEADS // 2
    first_head = lax.broadcasted_iota(jnp.int32, (lanes, lanes), 1) < head_dim
    frame_at = (lax.broadcasted_iota(jnp.int32, (patches, 2 * lanes), 1) % lanes) // patches
    for pair in range(pairs):
        start = pair * lanes
        weight = jnp.concatenate(
            [qkv_ref[:, start : start + lanes], qkv_ref[:, width + start : width + start + lanes]],
            axis=1,
        )
        packed = dot(normed_ref[...], weight).astype(jnp.bfloat16)
        for block in range(blocks):
            query = packed[block * lanes : (block + 1) * lanes, :lanes]
            key = packed[block * lanes : (block + 1) * lanes, lanes:]
            zero = jnp.zeros_like(key)
            keys = jnp.concatenate(
                [jnp.where(first_head, key, zero), jnp.where(first_head, zero, key)], axis=0
            )
            scores = dot_rows(query, keys)
            own_scores = scores[:patches]
            for frame in range(1, lanes // patches):
                own_scores = jnp.where(
                    frame_at == frame, scores[frame * patches : (frame + 1) * patches], own_scores
                )
            scores_ref[block, pair] = own_scores

    ones_row = lax.broadcasted_iota(jnp.int32, (2 * lanes, 2 * lanes), 0) // patches
    ones_column = lax.broadcasted_iota(jnp.int32, (2 * lanes, 2 * lanes), 1) // patches
    frame_ones = (ones_row == ones_column).astype(jnp.bfloat16)
    exp_scores = jnp.exp2(
        scores_ref[...].reshape(blocks * pairs * patches, 2 * lanes) * exponent
    )
    totals = dot(exp_scores.astype(jnp.bfloat16), frame_ones)
    probs = (exp_scores / totals).reshape(blocks * pairs, patches, 2 * lanes)
    sums = jnp.sum(probs, axis=1)
    key_sums = [
        jnp.concatenate(
            [
                sums[block * pairs : (block + 1) * pairs, side * lanes : (side + 1) * lanes]
                for block in range(blocks)
            ],
            axis=1,
        )
        for side in range(2)
    ]
    own = lax.broadcasted_iota(jnp.int32, (cands, rows), 1) // tokens == lax.broadcasted_iota(
        jnp.int32, (cands, rows), 0
    )
    spread = jnp.concatenate(
        [jnp.where(own, key_sums[head % 2][head // 2 : head // 2 + 1], 0.0) for head in range(HEADS)], axis=0
    ).astype(jnp.bfloat16)
    mixed_rows = dot(spread, normed_ref[...])
    for head in range(HEADS):
        mixed_rows_ref[head, pl.ds(pl.multiple_of(group * cands, cands), cands), :] = mixed_rows[
            head * cands : (head + 1) * cands
        ]

    @pl.when(group == pl.num_programs(0) - 1)
    def _():
        for copy in copies[2:]:
            copy.wait()
        total = pooled_ref.shape[0]
        quad = 4
        span = quad * head_dim
        pieces = []
        for part in range(HEADS // quad):
            left = mixed_rows_ref[pl.ds(part * quad, quad)].reshape(quad * total, width)
            both = dot_split(left, qkv_ref[:, pl.ds(2 * width + part * span, span)])
            head_at = lax.broadcasted_iota(jnp.int32, (total, span), 1) // head_dim
            piece = jnp.zeros((total, span), jnp.float32)
            for head in range(quad):
                piece = jnp.where(head_at == head, both[head * total : (head + 1) * total], piece)
            pieces.append(piece)
        mixed_mean = jnp.concatenate(pieces, axis=1) * (1.0 / tokens)
        hidden = sums_ref[...] * (1.0 / tokens) + dot_split(mixed_mean, out_ref[...])
        pooled = layer_norm(hidden).astype(jnp.bfloat16)
        pooled_ref[...] = pooled
        embedded_ref[...] = dot(pooled, proj_ref[...]).astype(jnp.bfloat16)


def encode_block(frames, qkv_weight, out_weight, proj_weight):
    cand_count, tokens, width = frames.shape
    key_width = proj_weight.shape[1]
    cands = 8
    rows = cands * tokens
    lanes = 2 * width // HEADS
    patches = tokens // FRAMES
    return pl.pallas_call(
        functools.partial(encode_kernel, tokens),
        grid=(cand_count // cands,),
        in_specs=[
            pl.BlockSpec((rows, width), lambda group: (group, 0)),
            pl.BlockSpec(memory_space=pl.ANY),
            pl.BlockSpec(memory_space=pl.ANY),
            pl.BlockSpec(memory_space=pl.ANY),
        ],
        out_specs=[
            pl.BlockSpec((cand_count, width), lambda group: (0, 0)),
            pl.BlockSpec((cand_count, key_width), lambda group: (0, 0)),
        ],
        out_shape=[
            jax.ShapeDtypeStruct((cand_count, width), jnp.bfloat16),
            jax.ShapeDtypeStruct((cand_count, key_width), jnp.bfloat16),
        ],
        scratch_shapes=[
            pltpu.VMEM(qkv_weight.shape, jnp.bfloat16),
            pltpu.VMEM(out_weight.shape, jnp.bfloat16),
            pltpu.VMEM(proj_weight.shape, jnp.bfloat16),
            pltpu.SemaphoreType.DMA((5,)),
            pltpu.VMEM((rows, width), jnp.bfloat16),
            pltpu.VMEM((rows * FRAMES // tokens * patches // lanes, HEADS // 2, patches, 2 * lanes), jnp.float32),
            pltpu.VMEM((HEADS, cand_count, width), jnp.float32),
            pltpu.VMEM((cand_count, width), jnp.float32),
        ],
        compiler_params=pltpu.CompilerParams(vmem_limit_bytes=60 * MIB),
        cost_estimate=pl.CostEstimate(
            flops=5 * cand_count * tokens * width * width, bytes_accessed=1 << 24, transcendentals=0
        ),
        name="encode",
    )(frames.reshape(cand_count * tokens, width), qkv_weight, out_weight, proj_weight)


def attend_kernel(
    inv_ref,
    slots_ref,
    near_ref,
    far_ref,
    history_ref,
    usable_ref,
    queries_ref,
    attended_ref,
    slope_ref,
):
    slots = slots_ref[...]
    half, key_width = near_ref.shape
    places = lax.broadcasted_iota(jnp.int32, (slots.shape[0], half), 1)
    queries = dot((slots == places).astype(jnp.bfloat16), near_ref[...])
    queries += dot((slots == places + half).astype(jnp.bfloat16), far_ref[...])
    queries = queries.astype(jnp.bfloat16)
    queries_ref[...] = queries
    events = history_ref.shape[0]
    chunk = math.gcd(events, 512)
    attended = jnp.zeros(attended_ref.shape, jnp.float32)
    for at in range(0, events, chunk):
        keys = history_ref[at : at + chunk, :]
        half_gate = 0.5 * jnp.tanh(dot_rows(queries, keys) * (0.5 / math.sqrt(key_width)))
        weights = (0.5 + half_gate) * usable_ref[:, at : at + chunk]
        slope_ref[:, at : at + chunk] = (weights * (0.5 - half_gate)).astype(jnp.bfloat16)
        attended += dot(weights.astype(jnp.bfloat16), keys)
    attended_ref[...] = attended * inv_ref[pl.program_id(0)]


def attend(inv_count, slots, near, far, history, usable):
    users, events, key_width = history.shape
    requests = slots.shape[0]
    per_user = requests // users
    return pl.pallas_call(
        attend_kernel,
        grid=(users,),
        in_specs=[
            pl.BlockSpec(memory_space=pltpu.SMEM),
            pl.BlockSpec((per_user, 1), lambda user: (user, 0)),
            pl.BlockSpec(near.shape, lambda user: (0, 0)),
            pl.BlockSpec(far.shape, lambda user: (0, 0)),
            pl.BlockSpec((None, events, key_width), lambda user: (user, 0, 0)),
            pl.BlockSpec((None, 1, events), lambda user: (user, 0, 0)),
        ],
        out_specs=[
            pl.BlockSpec((per_user, key_width), lambda user: (user, 0)),
            pl.BlockSpec((per_user, key_width), lambda user: (user, 0)),
            pl.BlockSpec((per_user, events), lambda user: (user, 0)),
        ],
        out_shape=[
            jax.ShapeDtypeStruct((requests, key_width), jnp.bfloat16),
            jax.ShapeDtypeStruct((requests, key_width), jnp.float32),
            jax.ShapeDtypeStruct((requests, events), jnp.bfloat16),
        ],
        compiler_params=pltpu.CompilerParams(vmem_limit_bytes=24 * MIB),
        cost_estimate=pl.CostEstimate(
            flops=4 * requests * events * key_width, bytes_accessed=1 << 24, transcendentals=0
        ),
        name="attend",
    )(inv_count, slots, near, far, history, usable)


def score_kernel(
    inv_ref,
    queries_ref,
    attended_ref,
    labels_ref,
    mlp_ref,
    logit_weight_ref,
    logits_ref,
    grad_att_ref,
    direct_ref,
):
    step_users = inv_ref.shape[0] // pl.num_programs(0)
    per_user = queries_ref.shape[0] // step_users
    query_b = queries_ref[...]
    query_f = query_b.astype(jnp.float32)
    attended = attended_ref[...]
    key_width = query_f.shape[1]
    joined = jnp.concatenate(
        [query_b, attended.astype(jnp.bfloat16), (query_f * attended).astype(jnp.bfloat16)], axis=1
    )
    pre_act = dot(joined, mlp_ref[...])
    act_sig = 0.5 * jnp.tanh(0.5 * pre_act) + 0.5
    hidden_units = (pre_act * act_sig).astype(jnp.bfloat16)
    weight = logit_weight_ref[...].astype(jnp.float32)
    logits = jnp.sum(hidden_units.astype(jnp.float32) * weight, axis=1, keepdims=True)
    logits_ref[...] = logits
    dlogit = (0.5 * jnp.tanh(0.5 * logits) + 0.5) - labels_ref[...].astype(jnp.float32)
    grad_pre = (dlogit * weight * (act_sig * (1.0 + pre_act * (1.0 - act_sig)))).astype(jnp.bfloat16)
    djoined = dot_rows(grad_pre, mlp_ref[...])
    part_query = djoined[:, :key_width]
    part_att = djoined[:, key_width : 2 * key_width]
    part_prod = djoined[:, 2 * key_width :]
    grad_att = part_att + part_prod * query_f
    for user in range(step_users):
        rows = slice(user * per_user, (user + 1) * per_user)
        inv_count = inv_ref[pl.program_id(0) * step_users + user]
        grad_att_ref[rows, :] = (grad_att[rows] * inv_count).astype(jnp.bfloat16)
    direct_ref[...] = part_query + part_prod * attended


def score(inv_count, queries, attended, labels, mlp_weight, logit_weight):
    users = inv_count.shape[0]
    requests, key_width = queries.shape
    steps = math.gcd(users, 2)
    step_rows = requests // steps
    block = pl.BlockSpec((step_rows, key_width), lambda step: (step, 0))
    column = pl.BlockSpec((step_rows, 1), lambda step: (step, 0))
    return pl.pallas_call(
        score_kernel,
        grid=(steps,),
        in_specs=[
            pl.BlockSpec(memory_space=pltpu.SMEM),
            block,
            block,
            column,
            pl.BlockSpec(mlp_weight.shape, lambda step: (0, 0)),
            pl.BlockSpec(logit_weight.shape, lambda step: (0, 0)),
        ],
        out_specs=[column, block, block],
        out_shape=[
            jax.ShapeDtypeStruct((requests, 1), jnp.float32),
            jax.ShapeDtypeStruct((requests, key_width), jnp.bfloat16),
            jax.ShapeDtypeStruct((requests, key_width), jnp.float32),
        ],
        compiler_params=pltpu.CompilerParams(vmem_limit_bytes=32 * MIB),
        cost_estimate=pl.CostEstimate(
            flops=4 * requests * mlp_weight.shape[0] * mlp_weight.shape[1],
            bytes_accessed=1 << 23,
            transcendentals=0,
        ),
        name="score",
    )(inv_count, queries, attended, labels, mlp_weight, logit_weight)


def attend_back_kernel(
    grad_att_ref, direct_ref, slope_ref, history_ref, grad_rows_ref
):
    grad_att = grad_att_ref[...]
    events, key_width = history_ref.shape
    chunk = math.gcd(events, 512)
    back = jnp.zeros(direct_ref.shape, jnp.float32)
    for at in range(0, events, chunk):
        keys = history_ref[at : at + chunk, :]
        slope = slope_ref[:, at : at + chunk].astype(jnp.float32)
        grad_sig = (dot_rows(grad_att, keys) * slope).astype(jnp.bfloat16)
        back += dot(grad_sig, keys)
    grad_rows_ref[...] = (direct_ref[...] + back * (1.0 / math.sqrt(key_width))).astype(jnp.bfloat16)


def attend_back(grad_att, direct, slope, history):
    users, events, key_width = history.shape
    requests = grad_att.shape[0]
    per_user = requests // users
    block = pl.BlockSpec((per_user, key_width), lambda user: (user, 0))
    return pl.pallas_call(
        attend_back_kernel,
        grid=(users,),
        in_specs=[
            block,
            block,
            pl.BlockSpec((per_user, events), lambda user: (user, 0)),
            pl.BlockSpec((None, events, key_width), lambda user: (user, 0, 0)),
        ],
        out_specs=block,
        out_shape=jax.ShapeDtypeStruct((requests, key_width), jnp.bfloat16),
        compiler_params=pltpu.CompilerParams(vmem_limit_bytes=20 * MIB),
        cost_estimate=pl.CostEstimate(
            flops=4 * requests * events * key_width, bytes_accessed=1 << 24, transcendentals=0
        ),
        name="attend_back",
    )(grad_att, direct, slope, history)


def terms_kernel(
    origins, me_ref, slots_ref, grad_rows_ref, near_ref, far_ref, keep_ref, send_ref, terms_ref
):
    half = near_ref.shape[0]
    requests = slots_ref.shape[1]
    grad_rows = grad_rows_ref[...]
    chunk = math.gcd(half, 512)
    steps = 0
    for offset, pooled_ref in ((0, near_ref), (half, far_ref)):
        for at in range(0, half, chunk):
            places = lax.broadcasted_iota(jnp.int32, (chunk, requests), 0) + (offset + at)
            row_hot = (places == slots_ref[...]).astype(jnp.bfloat16)
            cand_grad = dot(row_hot, grad_rows).astype(jnp.bfloat16)
            term = dot_columns(pooled_ref[at : at + chunk, :], cand_grad)
            if steps == 0:
                terms_ref[...] = term
            else:
                terms_ref[...] += term
            steps += 1
    rows = terms_ref.shape[0] // len(origins)
    me = me_ref[0]
    batch = max(1, 32 // rows)
    for slot in range(0, len(origins), batch):
        found = [
            terms_ref[pl.ds(pl.multiple_of((me ^ origins[slot + i]) * rows, rows), rows), :]
            for i in range(batch)
        ]
        found = found[0] if batch == 1 else jnp.concatenate(found, axis=0)
        out_ref, at = (keep_ref, slot) if slot < len(origins) // 2 else (send_ref, slot - len(origins) // 2)
        out_ref[at * rows : (at + batch) * rows, :] = found.astype(jnp.bfloat16)


def own_terms(origins, me, slots, grad_rows, near, far):
    width, key_width = near.shape[1], grad_rows.shape[1]
    whole = pl.BlockSpec(memory_space=pltpu.VMEM)
    return pl.pallas_call(
        functools.partial(terms_kernel, origins),
        in_specs=[pl.BlockSpec(memory_space=pltpu.SMEM), whole, whole, whole, whole],
        out_specs=[whole, whole],
        out_shape=[jax.ShapeDtypeStruct((width // 2, key_width), jnp.bfloat16)] * 2,
        scratch_shapes=[pltpu.VMEM((width, key_width), jnp.float32)],
        compiler_params=pltpu.CompilerParams(vmem_limit_bytes=20 * MIB),
        cost_estimate=pl.CostEstimate(
            flops=4 * near.shape[0] * key_width * (width + grad_rows.shape[0]),
            bytes_accessed=1 << 23,
            transcendentals=0,
        ),
        name="own_terms",
    )(me, slots, grad_rows, near, far)


def bit_groups(size):
    groups = []
    bit = 0
    while (1 << bit) < size:
        values = min(4, size >> bit)
        groups.append((bit, values))
        bit += values.bit_length() - 1
    return groups


def exchange(values, axis_name, size, distance):
    return lax.ppermute(values, axis_name, [(i, i ^ distance) for i in range(size)])


def gather_stage(rows, wides, bit, values):
    found = [exchange(rows, "wide", wides, step << bit) for step in range(1, values)]
    return jnp.concatenate([rows] + found, axis=0)


def after(values, *others):
    return lax.optimization_barrier((values,) + others)[0]


def slot_of(distance, wides):
    slot = 0
    for bit, values in bit_groups(wides):
        slot = slot * values + ((distance >> bit) & (values - 1))
    return slot + (distance // wides) * wides


def sum_blocks(keep, send, wides):
    total = keep.astype(jnp.float32) + exchange(send, "section", 2, 1).astype(jnp.float32)
    for bit, values in bit_groups(wides):
        parts = total.astype(jnp.bfloat16).reshape((values, -1) + keep.shape[1:])
        found = [
            exchange(parts[step], "wide", wides, step << bit).astype(jnp.float32)
            for step in range(1, values)
        ]
        total = sum(found, parts[0].astype(jnp.float32))
    return total


def body(
    frames,
    qkv_weight,
    out_weight,
    proj_weight,
    mlp_weight,
    logit_weight,
    history,
    hist_len,
    hist_mask,
    req_owner,
    req_local,
    labels,
):
    wides = lax.axis_size("wide")
    devices = lax.axis_size("section") * wides
    me = lax.axis_index("section") * wides + lax.axis_index("wide")
    cand_count = frames.shape[0]
    requests = req_local.shape[0]
    users, events, _ = history.shape
    pooled, embedded = encode_block(frames, qkv_weight, out_weight, proj_weight)
    positions = jnp.arange(events, dtype=jnp.int32)[None, :]
    usable = (
        (positions < hist_len[:, None]) & ((hist_mask == 1) | (positions == 0))
    ).astype(jnp.float32)
    inv_count = lax.rsqrt(jnp.sum(usable, axis=1))
    usable = usable.reshape(users, 1, events)
    slots = slot_of(req_owner[:, 0] ^ me, wides) * cand_count + req_local
    stages = list(reversed(bit_groups(wides)))
    near_embedded = embedded
    for bit, values in stages:
        near_embedded = gather_stage(near_embedded, wides, bit, values)
    far_embedded = exchange(near_embedded, "section", 2, 1)
    near_pooled = gather_stage(after(pooled, near_embedded), wides, *stages[0])
    queries, attended, slope = attend(
        inv_count, slots.reshape(requests, 1), near_embedded, far_embedded, history, usable
    )
    near_pooled = after(near_pooled, attended)
    for bit, values in stages[1:]:
        near_pooled = gather_stage(near_pooled, wides, bit, values)
    logits, grad_att, direct = score(
        inv_count,
        queries,
        attended,
        labels.reshape(requests, 1),
        mlp_weight,
        logit_weight.reshape(1, -1),
    )
    far_pooled = exchange(after(near_pooled, grad_att), "section", 2, 1)
    grad_rows = attend_back(grad_att, direct, slope, history)
    origins = [0] * devices
    for distance in range(devices):
        origins[slot_of(distance, wides)] = distance
    keep, send = own_terms(
        origins, me.reshape(1), slots.reshape(1, requests), grad_rows, near_pooled, far_pooled
    )
    grad_proj = sum_blocks(keep, send, wides)
    return (logits.reshape(requests), grad_proj)


def solution(mesh):
    in_specs = (
        P(("section", "wide"), None, None),
        P(),
        P(),
        P(),
        P(),
        P(),
        P(("section", "wide"), None, None),
        P(("section", "wide")),
        P(("section", "wide"), None),
        P(("section", "wide"), None),
        P(("section", "wide")),
        P(("section", "wide")),
    )
    out_specs = (P(("section", "wide")), P(("section", "wide"), None))
    return jax.shard_map(body, mesh=mesh, in_specs=in_specs, out_specs=out_specs, check_vma=False)
```

profile of v0, /device:TPU:0, one launch (start us, length us, event | category | flops | bytes accessed | tf_op | source)
XLA Modules:
  0.0 112.3 jit_solution(14113983535344492262)
XLA Ops:
  0.7 27.5 %encode.1 = (bf16[32,1024]{1,0:T(8,128)(2,1)}, bf16[32,512]{1,0:T(8,128)(2,1)}) custom-call(bf16[1536,1024]{1,0:T(8,128)(2,1)} %bitcast.4, bf16[1024,3072]{1,0:T(8,128)(2,1)} %qkv_hbm.1, bf16[1024,1024]{1,0:T(8,128)(2,1)} %out_hbm.1, bf16[1024,512]{1,0:T(8,128)(2,1)} %proj_hbm.1), custom_call_target="tpu_custom_call" | custom-call | flops 8053063680 | bytes 16777216 | tf_op jit(solution)/shard_map/encode/pallas_call | solution.py:188
  28.2 3.1 %collective-permute-start = (bf16[32,512]{1,0:T(8,128)(2,1)}, bf16[32,512]{1,0:T(8,128)(2,1)S(1)}, u32[]{:S(2)}, u32[]{:S(2)}) collective-permute-start(bf16[32,512]{1,0:T(8,128)(2,1)} %get-tuple-element.15), channel_id=1, source_target_pairs={{0,4},{1,5},{2,6},{3,7},{4,0},{5,1},{6,2},{7,3},{8,12},{9,13},{10,... | collective-permute-start | bytes 98312 | tf_op jit(solution)/shard_map/ppermute | solution.py:461
  31.3 2.6 %collective-permute-start.1 = (bf16[32,512]{1,0:T(8,128)(2,1)}, bf16[32,512]{1,0:T(8,128)(2,1)S(1)}, u32[]{:S(2)}, u32[]{:S(2)}) collective-permute-start(bf16[32,512]{1,0:T(8,128)(2,1)} %get-tuple-element.15), channel_id=1, source_target_pairs={{0,8},{1,9},{2,10},{3,11},{4,12},{5,13},{6,14},{7,15},{8,0},{9,1},... | collective-permute-start | bytes 98312 | tf_op jit(solution)/shard_map/ppermute | solution.py:461
  34.7 2.2 %collective-permute-done.1 = bf16[32,512]{1,0:T(8,128)(2,1)S(1)} collective-permute-done((bf16[32,512]{1,0:T(8,128)(2,1)}, bf16[32,512]{1,0:T(8,128)(2,1)S(1)}, u32[]{:S(2)}, u32[]{:S(2)}) %collective-permute-start.1) | collective-permute-done | bytes 32800 | tf_op jit(solution)/shard_map/ppermute | solution.py:461
  36.9 2.9 %collective-permute-done.2 = bf16[32,512]{1,0:T(8,128)(2,1)S(1)} collective-permute-done((bf16[32,512]{1,0:T(8,128)(2,1)}, bf16[32,512]{1,0:T(8,128)(2,1)S(1)}, u32[]{:S(2)}, u32[]{:S(2)}) %collective-permute-start.2) | collective-permute-done | bytes 32800 | tf_op jit(solution)/shard_map/ppermute | solution.py:461
  41.3 1.6 %collective-permute-start.4 = (bf16[128,512]{1,0:T(8,128)(2,1)S(1)}, bf16[128,512]{1,0:T(8,128)(2,1)S(1)}, u32[]{:S(2)}, u32[]{:S(2)}) collective-permute-start(bf16[128,512]{1,0:T(8,128)(2,1)S(1)} %get-tuple-element.36), channel_id=1, source_target_pairs={{0,2},{1,3},{2,0},{3,1},{4,6},{5,7},{6,4},{7,5},{8,10},{9,11},{10,... | collective-permute-start | bytes 393224 | tf_op jit(solution)/shard_map/ppermute | solution.py:461
  43.4 2.5 %collective-permute-done.3 = bf16[128,512]{1,0:T(8,128)(2,1)S(1)} collective-permute-done((bf16[128,512]{1,0:T(8,128)(2,1)S(1)}, bf16[128,512]{1,0:T(8,128)(2,1)S(1)}, u32[]{:S(2)}, u32[]{:S(2)}) %collective-permute-start.3) | collective-permute-done | bytes 131104 | tf_op jit(solution)/shard_map/ppermute | solution.py:461
  47.2 1.6 %collective-permute-done.5 = bf16[128,512]{1,0:T(8,128)(2,1)S(1)} collective-permute-done((bf16[128,512]{1,0:T(8,128)(2,1)S(1)}, bf16[128,512]{1,0:T(8,128)(2,1)S(1)}, u32[]{:S(2)}, u32[]{:S(2)}) %collective-permute-start.5) | collective-permute-done | bytes 131104 | tf_op jit(solution)/shard_map/ppermute | solution.py:461
  49.6 3.9 %collective-permute-start.7 = (bf16[32,1024]{1,0:T(8,128)(2,1)}, bf16[32,1024]{1,0:T(8,128)(2,1)S(1)}, u32[]{:S(2)}, u32[]{:S(2)}) collective-permute-start(bf16[32,1024]{1,0:T(8,128)(2,1)} %get-tuple-element.23), channel_id=1, source_target_pairs={{0,4},{1,5},{2,6},{3,7},{4,0},{5,1},{6,2},{7,3},{8,12},{9,13},{10,... | collective-permute-start | bytes 196616 | tf_op jit(solution)/shard_map/ppermute | solution.py:461
  53.9 2.2 %collective-permute-done.9 = bf16[32,1024]{1,0:T(8,128)(2,1)S(1)} collective-permute-done((bf16[32,1024]{1,0:T(8,128)(2,1)}, bf16[32,1024]{1,0:T(8,128)(2,1)S(1)}, u32[]{:S(2)}, u32[]{:S(2)}) %collective-permute-start.9) | collective-permute-done | bytes 65568 | tf_op jit(solution)/shard_map/ppermute | solution.py:461
  56.1 1.6 %collective-permute-done.8 = bf16[32,1024]{1,0:T(8,128)(2,1)S(1)} collective-permute-done((bf16[32,1024]{1,0:T(8,128)(2,1)}, bf16[32,1024]{1,0:T(8,128)(2,1)S(1)}, u32[]{:S(2)}, u32[]{:S(2)}) %collective-permute-start.8) | collective-permute-done | bytes 65568 | tf_op jit(solution)/shard_map/ppermute | solution.py:461
  58.6 3.4 %copy-done = bf16[4,2048,512]{2,1,0:T(8,128)(2,1)S(1)} copy-done((bf16[4,2048,512]{2,1,0:T(8,128)(2,1)S(1)}, bf16[4,2048,512]{2,1,0:T(8,128)(2,1)}, u32[]{:S(2)}) %copy-start) | copy-done | bytes 8388632
  61.9 8.4 %attend.1 = (bf16[768,512]{1,0:T(8,128)(2,1)S(1)}, f32[768,512]{1,0:T(8,128)S(1)}, bf16[768,2048]{1,0:T(8,128)(2,1)S(1)}) custom-call(f32[4]{0:T(128)S(1)} %rsqrt.3.inv_ref, s32[768,1]{1,0:T(8,128)S(1)} %reshape.62.slots_ref, bf16[512,512]{1,0:T(8,128)(2,1)S(1)} %constant_dynamic-update-slice_fusion.4.near_ref, ...), custom_call_target="tpu_custom_call" | custom-call | flops 3221225472 | bytes 16777216 | tf_op jit(solution)/shard_map/attend/pallas_call | solution.py:257
  71.5 2.4 %collective-permute-start.12 = (bf16[128,1024]{1,0:T(8,128)(2,1)S(1)}, bf16[128,1024]{1,0:T(8,128)(2,1)S(1)}, u32[]{:S(2)}, u32[]{:S(2)}) collective-permute-start(bf16[128,1024]{1,0:T(8,128)(2,1)S(1)} %pad_maximum_fusion), channel_id=1, source_target_pairs={{0,3},{1,2},{2,1},{3,0},{4,7},{5,6},{6,5},{7,4},{8,11},{9,10},{10,... | collective-permute-start | bytes 786440 | tf_op jit(solution)/shard_map/ppermute | solution.py:461
  73.9 7.5 %score.1 = (f32[768,1]{1,0:T(8,128)S(1)}, bf16[768,512]{1,0:T(8,128)(2,1)S(1)}, f32[768,512]{1,0:T(8,128)S(1)}) custom-call(f32[4]{0:T(128)S(1)} %rsqrt.3.inv_ref, bf16[768,512]{1,0:T(8,128)(2,1)S(1)} %get-tuple-element.16.queries_ref, f32[768,512]{1,0:T(8,128)S(1)} %get-tuple-element.17.attended_ref, s32[768,1]{1,0:T(8,128)S(1)} %reshape.63.labels_ref, ...), custom_call_target="tpu_custom_call" | custom-call | flops 4831838208 | bytes 8388608 | tf_op jit(solution)/shard_map/score/pallas_call | solution.py:333
  81.5 2.8 %collective-permute-done.12 = bf16[128,1024]{1,0:T(8,128)(2,1)S(1)} collective-permute-done((bf16[128,1024]{1,0:T(8,128)(2,1)S(1)}, bf16[128,1024]{1,0:T(8,128)(2,1)S(1)}, u32[]{:S(2)}, u32[]{:S(2)}) %collective-permute-start.12) | collective-permute-done | bytes 262176 | tf_op jit(solution)/shard_map/ppermute | solution.py:461
  84.5 6.2 %attend_back.1.grad_rows_ref = bf16[768,512]{1,0:T(8,128)(2,1)S(1)} custom-call(bf16[768,512]{1,0:T(8,128)(2,1)S(1)} %get-tuple-element.19.grad_att_ref, f32[768,512]{1,0:T(8,128)S(1)} %get-tuple-element.20.direct_ref, bf16[768,2048]{1,0:T(8,128)(2,1)S(1)} %get-tuple-element.21.slope_ref, bf16[4,2048,512]{2,1,0:T(8,128)(2,1)S(1)} %bitcast.3), custom_call_target="tpu_custom_call" | custom-call | flops 3221225472 | bytes 16777216 | tf_op jit(solution)/shard_map/attend_back/pallas_call | solution.py:380
  90.6 2.3 %own_terms.1 = (bf16[512,512]{1,0:T(8,128)(2,1)S(1)}, bf16[512,512]{1,0:T(8,128)(2,1)S(1)}) custom-call(s32[1]{0:T(128)} %bitcast.1.me_ref, s32[1,768]{1,0:T(1,128)S(1)} %reshape.61.slots_ref, bf16[768,512]{1,0:T(8,128)(2,1)S(1)} %attend_back.1.grad_rows_ref, bf16[512,1024]{1,0:T(8,128)(2,1)S(1)} %constant_dynamic-update-slice_fusion.11.near_ref, ...), custom_call_target="tpu_custom_call" | custom-call | flops 1879048192 | bytes 8388608 | tf_op jit(solution)/shard_map/own_terms/pallas_call | solution.py:434
  93.5 1.5 %collective-permute-done.14 = bf16[512,512]{1,0:T(8,128)(2,1)S(1)} collective-permute-done((bf16[512,512]{1,0:T(8,128)(2,1)S(1)}, bf16[512,512]{1,0:T(8,128)(2,1)S(1)}, u32[]{:S(2)}, u32[]{:S(2)}) %collective-permute-start.14) | collective-permute-done | bytes 524320 | tf_op jit(solution)/shard_map/ppermute | solution.py:461
  95.2 1.8 %collective-permute-start.17 = (bf16[128,512]{1,0:T(8,128)(2,1)S(1)}, bf16[128,512]{1,0:T(8,128)(2,1)S(1)}, u32[]{:S(2)}, u32[]{:S(2)}) collective-permute-start(bf16[128,512]{1,0:T(8,128)(2,1)S(1)} %get-tuple-element.31), channel_id=1, source_target_pairs={{0,3},{1,2},{2,1},{3,0},{4,7},{5,6},{6,5},{7,4},{8,11},{9,10},{10,... | collective-permute-start | bytes 393224 | tf_op jit(solution)/shard_map/ppermute | solution.py:461
  98.8 3.7 %collective-permute-done.17 = bf16[128,512]{1,0:T(8,128)(2,1)S(1)} collective-permute-done((bf16[128,512]{1,0:T(8,128)(2,1)S(1)}, bf16[128,512]{1,0:T(8,128)(2,1)S(1)}, u32[]{:S(2)}, u32[]{:S(2)}) %collective-permute-start.17) | collective-permute-done | bytes 131104 | tf_op jit(solution)/shard_map/ppermute | solution.py:461
  102.5 2.2 %collective-permute-done.16 = bf16[128,512]{1,0:T(8,128)(2,1)S(1)} collective-permute-done((bf16[128,512]{1,0:T(8,128)(2,1)S(1)}, bf16[128,512]{1,0:T(8,128)(2,1)S(1)}, u32[]{:S(2)}, u32[]{:S(2)}) %collective-permute-start.16) | collective-permute-done | bytes 131104 | tf_op jit(solution)/shard_map/ppermute | solution.py:461
  104.9 1.7 %collective-permute-start.20 = (bf16[32,512]{1,0:T(8,128)(2,1)S(1)}, bf16[32,512]{1,0:T(8,128)(2,1)S(1)}, u32[]{:S(2)}, u32[]{:S(2)}) collective-permute-start(bf16[32,512]{1,0:T(8,128)(2,1)S(1)} %get-tuple-element.34), channel_id=1, source_target_pairs={{0,12},{1,13},{2,14},{3,15},{4,8},{5,9},{6,10},{7,11},{8,4},{9,5},... | collective-permute-start | bytes 98312 | tf_op jit(solution)/shard_map/ppermute | solution.py:461
  106.5 2.8 %collective-permute-start.18 = (bf16[32,512]{1,0:T(8,128)(2,1)S(1)}, bf16[32,512]{1,0:T(8,128)(2,1)S(1)}, u32[]{:S(2)}, u32[]{:S(2)}) collective-permute-start(bf16[32,512]{1,0:T(8,128)(2,1)S(1)} %get-tuple-element.33), channel_id=1, source_target_pairs={{0,4},{1,5},{2,6},{3,7},{4,0},{5,1},{6,2},{7,3},{8,12},{9,13},{10,... | collective-permute-start | bytes 98312 | tf_op jit(solution)/shard_map/ppermute | solution.py:461
  (72 shorter events, 13.0 us)
Async XLA Ops:
  0.7 52.8 %copy-start.4 = (s32[768]{0:T(1024)S(1)}, s32[768]{0:T(1024)}, u32[]{:S(2)}) copy-start(s32[768]{0:T(1024)} %param.22) | copy-start | bytes 9220
  0.7 53.1 %copy-start.3 = (s32[768]{0:T(1024)S(1)}, s32[768]{0:T(1024)}, u32[]{:S(2)}) copy-start(s32[768]{0:T(1024)} %param.23) | copy-start | bytes 9220
  0.7 53.2 %copy-start.6 = (bf16[1024]{0:T(1024)(128)(2,1)S(1)}, bf16[1024]{0:T(1024)(128)(2,1)}, u32[]{:S(2)}) copy-start(bf16[1024]{0:T(1024)(128)(2,1)} %param.17) | copy-start | bytes 6148
  28.2 6.5 %collective-permute-start = (bf16[32,512]{1,0:T(8,128)(2,1)}, bf16[32,512]{1,0:T(8,128)(2,1)S(1)}, u32[]{:S(2)}, u32[]{:S(2)}) collective-permute-start(bf16[32,512]{1,0:T(8,128)(2,1)} %get-tuple-element.15), channel_id=1, source_target_pairs={{0,4},{1,5},{2,6},{3,7},{4,0},{5,1},{6,2},{7,3},{8,12},{9,13},{10,... | collective-permute-start | bytes 98312 | tf_op jit(solution)/shard_map/ppermute | solution.py:461
  31.3 5.6 %collective-permute-start.1 = (bf16[32,512]{1,0:T(8,128)(2,1)}, bf16[32,512]{1,0:T(8,128)(2,1)S(1)}, u32[]{:S(2)}, u32[]{:S(2)}) collective-permute-start(bf16[32,512]{1,0:T(8,128)(2,1)} %get-tuple-element.15), channel_id=1, source_target_pairs={{0,8},{1,9},{2,10},{3,11},{4,12},{5,13},{6,14},{7,15},{8,0},{9,1},... | collective-permute-start | bytes 98312 | tf_op jit(solution)/shard_map/ppermute | solution.py:461
  33.9 5.9 %collective-permute-start.2 = (bf16[32,512]{1,0:T(8,128)(2,1)}, bf16[32,512]{1,0:T(8,128)(2,1)S(1)}, u32[]{:S(2)}, u32[]{:S(2)}) collective-permute-start(bf16[32,512]{1,0:T(8,128)(2,1)} %get-tuple-element.15), channel_id=1, source_target_pairs={{0,12},{1,13},{2,14},{3,15},{4,8},{5,9},{6,10},{7,11},{8,4},{9,5},... | collective-permute-start | bytes 98312 | tf_op jit(solution)/shard_map/ppermute | solution.py:461
  39.8 6.1 %collective-permute-start.3 = (bf16[128,512]{1,0:T(8,128)(2,1)S(1)}, bf16[128,512]{1,0:T(8,128)(2,1)S(1)}, u32[]{:S(2)}, u32[]{:S(2)}) collective-permute-start(bf16[128,512]{1,0:T(8,128)(2,1)S(1)} %get-tuple-element.36), channel_id=1, source_target_pairs={{0,1},{1,0},{2,3},{3,2},{4,5},{5,4},{6,7},{7,6},{8,9},{9,8},{10,11... | collective-permute-start | bytes 393224 | tf_op jit(solution)/shard_map/ppermute | solution.py:461
  41.3 5.9 %collective-permute-start.4 = (bf16[128,512]{1,0:T(8,128)(2,1)S(1)}, bf16[128,512]{1,0:T(8,128)(2,1)S(1)}, u32[]{:S(2)}, u32[]{:S(2)}) collective-permute-start(bf16[128,512]{1,0:T(8,128)(2,1)S(1)} %get-tuple-element.36), channel_id=1, source_target_pairs={{0,2},{1,3},{2,0},{3,1},{4,6},{5,7},{6,4},{7,5},{8,10},{9,11},{10,... | collective-permute-start | bytes 393224 | tf_op jit(solution)/shard_map/ppermute | solution.py:461
  42.9 5.9 %collective-permute-start.5 = (bf16[128,512]{1,0:T(8,128)(2,1)S(1)}, bf16[128,512]{1,0:T(8,128)(2,1)S(1)}, u32[]{:S(2)}, u32[]{:S(2)}) collective-permute-start(bf16[128,512]{1,0:T(8,128)(2,1)S(1)} %get-tuple-element.36), channel_id=1, source_target_pairs={{0,3},{1,2},{2,1},{3,0},{4,7},{5,6},{6,5},{7,4},{8,11},{9,10},{10,... | collective-permute-start | bytes 393224 | tf_op jit(solution)/shard_map/ppermute | solution.py:461
  48.8 9.8 %collective-permute-start.6 = (bf16[512,512]{1,0:T(8,128)(2,1)S(1)}, bf16[512,512]{1,0:T(8,128)(2,1)S(1)}, u32[]{:S(2)}, u32[]{:S(2)}) collective-permute-start(bf16[512,512]{1,0:T(8,128)(2,1)S(1)} %constant_dynamic-update-slice_fusion.4.near_ref), channel_id=1, source_target_pairs={{0,16},{16,0},{1,17},{17,1},{2,18},{18,2},{3,19},{19,3},{4,20},{20... | collective-permute-start | bytes 1572872 | tf_op jit(solution)/shard_map/ppermute | solution.py:461
  49.1 7.1 %collective-permute-start.9 = (bf16[32,1024]{1,0:T(8,128)(2,1)}, bf16[32,1024]{1,0:T(8,128)(2,1)S(1)}, u32[]{:S(2)}, u32[]{:S(2)}) collective-permute-start(bf16[32,1024]{1,0:T(8,128)(2,1)} %get-tuple-element.23), channel_id=1, source_target_pairs={{0,12},{1,13},{2,14},{3,15},{4,8},{5,9},{6,10},{7,11},{8,4},{9,5},... | collective-permute-start | bytes 196616 | tf_op jit(solution)/shard_map/ppermute | solution.py:461
  49.5 8.2 %collective-permute-start.8 = (bf16[32,1024]{1,0:T(8,128)(2,1)}, bf16[32,1024]{1,0:T(8,128)(2,1)S(1)}, u32[]{:S(2)}, u32[]{:S(2)}) collective-permute-start(bf16[32,1024]{1,0:T(8,128)(2,1)} %get-tuple-element.23), channel_id=1, source_target_pairs={{0,8},{1,9},{2,10},{3,11},{4,12},{5,13},{6,14},{7,15},{8,0},{9,1},... | collective-permute-start | bytes 196616 | tf_op jit(solution)/shard_map/ppermute | solution.py:461
  49.6 8.1 %collective-permute-start.7 = (bf16[32,1024]{1,0:T(8,128)(2,1)}, bf16[32,1024]{1,0:T(8,128)(2,1)S(1)}, u32[]{:S(2)}, u32[]{:S(2)}) collective-permute-start(bf16[32,1024]{1,0:T(8,128)(2,1)} %get-tuple-element.23), channel_id=1, source_target_pairs={{0,4},{1,5},{2,6},{3,7},{4,0},{5,1},{6,2},{7,3},{8,12},{9,13},{10,... | collective-permute-start | bytes 196616 | tf_op jit(solution)/shard_map/ppermute | solution.py:461
  70.4 11.1 %collective-permute-start.10 = (bf16[128,1024]{1,0:T(8,128)(2,1)S(1)}, bf16[128,1024]{1,0:T(8,128)(2,1)S(1)}, u32[]{:S(2)}, u32[]{:S(2)}) collective-permute-start(bf16[128,1024]{1,0:T(8,128)(2,1)S(1)} %pad_maximum_fusion), channel_id=1, source_target_pairs={{0,1},{1,0},{2,3},{3,2},{4,5},{5,4},{6,7},{7,6},{8,9},{9,8},{10,11... | collective-permute-start | bytes 786440 | tf_op jit(solution)/shard_map/ppermute | solution.py:461
  70.9 10.6 %collective-permute-start.11 = (bf16[128,1024]{1,0:T(8,128)(2,1)S(1)}, bf16[128,1024]{1,0:T(8,128)(2,1)S(1)}, u32[]{:S(2)}, u32[]{:S(2)}) collective-permute-start(bf16[128,1024]{1,0:T(8,128)(2,1)S(1)} %pad_maximum_fusion), channel_id=1, source_target_pairs={{0,2},{1,3},{2,0},{3,1},{4,6},{5,7},{6,4},{7,5},{8,10},{9,11},{10,... | collective-permute-start | bytes 786440 | tf_op jit(solution)/shard_map/ppermute | solution.py:461
  71.5 12.8 %collective-permute-start.12 = (bf16[128,1024]{1,0:T(8,128)(2,1)S(1)}, bf16[128,1024]{1,0:T(8,128)(2,1)S(1)}, u32[]{:S(2)}, u32[]{:S(2)}) collective-permute-start(bf16[128,1024]{1,0:T(8,128)(2,1)S(1)} %pad_maximum_fusion), channel_id=1, source_target_pairs={{0,3},{1,2},{2,1},{3,0},{4,7},{5,6},{6,5},{7,4},{8,11},{9,10},{10,... | collective-permute-start | bytes 786440 | tf_op jit(solution)/shard_map/ppermute | solution.py:461
  84.3 6.3 %collective-permute-start.13 = (bf16[512,1024]{1,0:T(8,128)(2,1)S(1)}, bf16[512,1024]{1,0:T(8,128)(2,1)S(1)}, u32[]{:S(2)}, u32[]{:S(2)}) collective-permute-start(bf16[512,1024]{1,0:T(8,128)(2,1)S(1)} %constant_dynamic-update-slice_fusion.11.near_ref), channel_id=1, source_target_pairs={{0,16},{16,0},{1,17},{17,1},{2,18},{18,2},{3,19},{19,3},{4,20},{20... | collective-permute-start | bytes 3145736 | tf_op jit(solution)/shard_map/ppermute | solution.py:461
  93.0 2.1 %collective-permute-start.14 = (bf16[512,512]{1,0:T(8,128)(2,1)S(1)}, bf16[512,512]{1,0:T(8,128)(2,1)S(1)}, u32[]{:S(2)}, u32[]{:S(2)}) collective-permute-start(bf16[512,512]{1,0:T(8,128)(2,1)S(1)} %get-tuple-element.27), channel_id=1, source_target_pairs={{0,16},{16,0},{1,17},{17,1},{2,18},{18,2},{3,19},{19,3},{4,20},{20... | collective-permute-start | bytes 1572872 | tf_op jit(solution)/shard_map/ppermute | solution.py:461
  95.2 7.3 %collective-permute-start.17 = (bf16[128,512]{1,0:T(8,128)(2,1)S(1)}, bf16[128,512]{1,0:T(8,128)(2,1)S(1)}, u32[]{:S(2)}, u32[]{:S(2)}) collective-permute-start(bf16[128,512]{1,0:T(8,128)(2,1)S(1)} %get-tuple-element.31), channel_id=1, source_target_pairs={{0,3},{1,2},{2,1},{3,0},{4,7},{5,6},{6,5},{7,4},{8,11},{9,10},{10,... | collective-permute-start | bytes 393224 | tf_op jit(solution)/shard_map/ppermute | solution.py:461
  97.1 7.7 %collective-permute-start.16 = (bf16[128,512]{1,0:T(8,128)(2,1)S(1)}, bf16[128,512]{1,0:T(8,128)(2,1)S(1)}, u32[]{:S(2)}, u32[]{:S(2)}) collective-permute-start(bf16[128,512]{1,0:T(8,128)(2,1)S(1)} %get-tuple-element.32), channel_id=1, source_target_pairs={{0,2},{1,3},{2,0},{3,1},{4,6},{5,7},{6,4},{7,5},{8,10},{9,11},{10,... | collective-permute-start | bytes 393224 | tf_op jit(solution)/shard_map/ppermute | solution.py:461
  98.2 6.5 %collective-permute-start.15 = (bf16[128,512]{1,0:T(8,128)(2,1)S(1)}, bf16[128,512]{1,0:T(8,128)(2,1)S(1)}, u32[]{:S(2)}, u32[]{:S(2)}) collective-permute-start(bf16[128,512]{1,0:T(8,128)(2,1)S(1)} %get-tuple-element.30), channel_id=1, source_target_pairs={{0,1},{1,0},{2,3},{3,2},{4,5},{5,4},{6,7},{7,6},{8,9},{9,8},{10,11... | collective-permute-start | bytes 393224 | tf_op jit(solution)/shard_map/ppermute | solution.py:461
  104.9 5.8 %collective-permute-start.20 = (bf16[32,512]{1,0:T(8,128)(2,1)S(1)}, bf16[32,512]{1,0:T(8,128)(2,1)S(1)}, u32[]{:S(2)}, u32[]{:S(2)}) collective-permute-start(bf16[32,512]{1,0:T(8,128)(2,1)S(1)} %get-tuple-element.34), channel_id=1, source_target_pairs={{0,12},{1,13},{2,14},{3,15},{4,8},{5,9},{6,10},{7,11},{8,4},{9,5},... | collective-permute-start | bytes 98312 | tf_op jit(solution)/shard_map/ppermute | solution.py:461
  106.5 5.0 %collective-permute-start.19 = (bf16[32,512]{1,0:T(8,128)(2,1)S(1)}, bf16[32,512]{1,0:T(8,128)(2,1)S(1)}, u32[]{:S(2)}, u32[]{:S(2)}) collective-permute-start(bf16[32,512]{1,0:T(8,128)(2,1)S(1)} %get-tuple-element.35), channel_id=1, source_target_pairs={{0,8},{1,9},{2,10},{3,11},{4,12},{5,13},{6,14},{7,15},{8,0},{9,1},... | collective-permute-start | bytes 98312 | tf_op jit(solution)/shard_map/ppermute | solution.py:461
  106.5 5.1 %collective-permute-start.18 = (bf16[32,512]{1,0:T(8,128)(2,1)S(1)}, bf16[32,512]{1,0:T(8,128)(2,1)S(1)}, u32[]{:S(2)}, u32[]{:S(2)}) collective-permute-start(bf16[32,512]{1,0:T(8,128)(2,1)S(1)} %get-tuple-element.33), channel_id=1, source_target_pairs={{0,4},{1,5},{2,6},{3,7},{4,0},{5,1},{6,2},{7,3},{8,12},{9,13},{10,... | collective-permute-start | bytes 98312 | tf_op jit(solution)/shard_map/ppermute | solution.py:461
  (7 other events, 173.4 us)
where the time goes:
time: 113 us; the launch traced here: 112 us
  Pallas kernels  51.9 us (46%)
  waiting for transfers between devices  26.1 us (23%)
  starting transfers between devices  25.9 us (23%)
  local copies, waits for them, and re-layouts  4.75 us (4%)
  other arithmetic  2.71 us (2%)
    pallas_call x1, Pallas kernels, encode_block(): pl.pallas_call(functools.partial(encode_kernel, tokens), grid=(cand_count...  27.5 us
    ppermute x21, waiting for transfers between devices, exchange(): lax.ppermute(values, axis_name, [(i, i ^ distance) for i in range(size)])  26.1 us
    ppermute x21, starting transfers between devices, exchange(): lax.ppermute(values, axis_name, [(i, i ^ distance) for i in range(size)])  25.9 us
    pallas_call x1, Pallas kernels, attend(): pl.pallas_call(attend_kernel, grid=(users,), in_specs=[pl.BlockSpec(memor...  8.42 us
    pallas_call x1, Pallas kernels, score(): pl.pallas_call(score_kernel, grid=(steps,), in_specs=[pl.BlockSpec(memory...  7.5 us
    pallas_call x1, Pallas kernels, attend_back(): pl.pallas_call(attend_back_kernel, grid=(users,), in_specs=[block, block,...  6.16 us
    unnamed x28, local copies, waits for them, and re-layouts  4.33 us
    pallas_call x1, Pallas kernels, own_terms(): pl.pallas_call(functools.partial(terms_kernel, origins), in_specs=[pl.Blo...  2.33 us
  transfers between devices with their start and end apart: 21, of which 14 were waited for; matrix products, arithmetic and copies ran while one was open for 3% of the time, Pallas kernels for 12%

commit v1 on v0

--- a/solution.py
+++ b/solution.py
@@ -48,7 +48,8 @@
 
 def encode_kernel(
     tokens,
-    frames_ref,
+    first_ref,
+    next_ref,
     qkv_hbm,
     out_hbm,
     proj_hbm,
@@ -64,7 +65,7 @@
     sums_ref,
 ):
     group = pl.program_id(0)
-    rows, width = normed_ref.shape
+    rows, width = next_ref.shape
     head_dim = width // HEADS
     patches = tokens // FRAMES
     cands = rows // tokens
@@ -86,17 +87,24 @@
         for copy in copies:
             copy.start()
 
-    inputs = frames_ref[...].astype(jnp.float32)
-    sums_ref[pl.ds(pl.multiple_of(group * cands, cands), cands), :] = jnp.sum(
-        inputs.reshape(cands, tokens, width), axis=1
-    )
-    normed_ref[...] = layer_norm(inputs).astype(jnp.bfloat16)
+    def norm_cand(source_ref, half, cand_group, cand):
+        at = cand * tokens
+        inputs = source_ref[at : at + tokens, :].astype(jnp.float32)
+        start = pl.multiple_of(half * rows, rows) + at
+        normed_ref[pl.ds(pl.multiple_of(start, tokens), tokens), :] = layer_norm(inputs).astype(
+            jnp.bfloat16
+        )
+        sums_ref[cand_group * cands + cand] = jnp.sum(inputs, axis=0, keepdims=True)
 
     @pl.when(group == 0)
     def _():
+        for cand in range(cands):
+            norm_cand(first_ref, 0, 0, cand)
         copies[0].wait()
         copies[1].wait()
 
+    place = pl.multiple_of((group % 2) * rows, rows)
+    following = jnp.minimum(group + 1, pl.num_programs(0) - 1)
     exponent = math.log2(math.e) / math.sqrt(head_dim)
     blocks = rows // lanes
     pairs = HEADS // 2
@@ -108,7 +116,7 @@
             [qkv_ref[:, start : start + lanes], qkv_ref[:, width + start : width + start + lanes]],
             axis=1,
         )
-        packed = dot(normed_ref[...], weight).astype(jnp.bfloat16)
+        packed = dot(normed_ref[pl.ds(place, rows), :], weight).astype(jnp.bfloat16)
         for block in range(blocks):
             query = packed[block * lanes : (block + 1) * lanes, :lanes]
             key = packed[block * lanes : (block + 1) * lanes, lanes:]
@@ -123,6 +131,8 @@
                     frame_at == frame, scores[frame * patches : (frame + 1) * patches], own_scores
                 )
             scores_ref[block, pair] = own_scores
+        if pair < cands:
+            norm_cand(next_ref, 1 - group % 2, following, pair)
 
     ones_row = lax.broadcasted_iota(jnp.int32, (2 * lanes, 2 * lanes), 0) // patches
     ones_column = lax.broadcasted_iota(jnp.int32, (2 * lanes, 2 * lanes), 1) // patches
@@ -149,7 +159,7 @@
     spread = jnp.concatenate(
         [jnp.where(own, key_sums[head % 2][head // 2 : head // 2 + 1], 0.0) for head in range(HEADS)], axis=0
     ).astype(jnp.bfloat16)
-    mixed_rows = dot(spread, normed_ref[...])
+    mixed_rows = dot(spread, normed_ref[pl.ds(place, rows), :])
     for head in range(HEADS):
         mixed_rows_ref[head, pl.ds(pl.multiple_of(group * cands, cands), cands), :] = mixed_rows[
             head * cands : (head + 1) * cands
@@ -172,7 +182,7 @@
                 piece = jnp.where(head_at == head, both[head * total : (head + 1) * total], piece)
             pieces.append(piece)
         mixed_mean = jnp.concatenate(pieces, axis=1) * (1.0 / tokens)
-        hidden = sums_ref[...] * (1.0 / tokens) + dot_split(mixed_mean, out_ref[...])
+        hidden = sums_ref[...].reshape(total, width) * (1.0 / tokens) + dot_split(mixed_mean, out_ref[...])
         pooled = layer_norm(hidden).astype(jnp.bfloat16)
         pooled_ref[...] = pooled
         embedded_ref[...] = dot(pooled, proj_ref[...]).astype(jnp.bfloat16)
@@ -183,13 +193,16 @@
     key_width = proj_weight.shape[1]
     cands = 8
     rows = cands * tokens
+    last = cand_count // cands - 1
+    rows_in = frames.reshape(cand_count * tokens, width)
     lanes = 2 * width // HEADS
     patches = tokens // FRAMES
     return pl.pallas_call(
         functools.partial(encode_kernel, tokens),
         grid=(cand_count // cands,),
         in_specs=[
-            pl.BlockSpec((rows, width), lambda group: (group, 0)),
+            pl.BlockSpec((rows, width), lambda group: (0, 0)),
+            pl.BlockSpec((rows, width), lambda group: (jnp.minimum(group + 1, last), 0)),
             pl.BlockSpec(memory_space=pl.ANY),
             pl.BlockSpec(memory_space=pl.ANY),
             pl.BlockSpec(memory_space=pl.ANY),
@@ -207,17 +220,17 @@
             pltpu.VMEM(out_weight.shape, jnp.bfloat16),
             pltpu.VMEM(proj_weight.shape, jnp.bfloat16),
             pltpu.SemaphoreType.DMA((5,)),
-            pltpu.VMEM((rows, width), jnp.bfloat16),
+            pltpu.VMEM((2 * rows, width), jnp.bfloat16),
             pltpu.VMEM((rows * FRAMES // tokens * patches // lanes, HEADS // 2, patches, 2 * lanes), jnp.float32),
             pltpu.VMEM((HEADS, cand_count, width), jnp.float32),
-            pltpu.VMEM((cand_count, width), jnp.float32),
+            pltpu.VMEM((cand_count, 1, width), jnp.float32),
         ],
         compiler_params=pltpu.CompilerParams(vmem_limit_bytes=60 * MIB),
         cost_estimate=pl.CostEstimate(
             flops=5 * cand_count * tokens * width * width, bytes_accessed=1 << 24, transcendentals=0
         ),
         name="encode",
-    )(frames.reshape(cand_count * tokens, width), qkv_weight, out_weight, proj_weight)
+    )(rows_in, rows_in, qkv_weight, out_weight, proj_weight)
 
 
 def attend_kernel(
@@ -275,7 +288,7 @@
             jax.ShapeDtypeStruct((requests, key_width), jnp.float32),
             jax.ShapeDtypeStruct((requests, events), jnp.bfloat16),
         ],
-        compiler_params=pltpu.CompilerParams(vmem_limit_bytes=24 * MIB),
+        compiler_params=pltpu.CompilerParams(vmem_limit_bytes=60 * MIB),
         cost_estimate=pl.CostEstimate(
             flops=4 * requests * events * key_width, bytes_accessed=1 << 24, transcendentals=0
         ),
@@ -397,7 +410,7 @@
 
 
 def terms_kernel(
-    origins, me_ref, slots_ref, grad_rows_ref, near_ref, far_ref, keep_ref, send_ref, terms_ref
+    origins, core_ref, slots_ref, grad_rows_ref, near_ref, far_ref, keep_ref, send_ref, terms_ref
 ):
     half = near_ref.shape[0]
     requests = slots_ref.shape[1]
@@ -416,11 +429,11 @@
                 terms_ref[...] += term
             steps += 1
     rows = terms_ref.shape[0] // len(origins)
-    me = me_ref[0]
+    core = core_ref[0]
     batch = max(1, 32 // rows)
     for slot in range(0, len(origins), batch):
         found = [
-            terms_ref[pl.ds(pl.multiple_of((me ^ origins[slot + i]) * rows, rows), rows), :]
+            terms_ref[pl.ds(pl.multiple_of((core ^ origins[slot + i]) * rows, rows), rows), :]
             for i in range(batch)
         ]
         found = found[0] if batch == 1 else jnp.concatenate(found, axis=0)
@@ -428,7 +441,7 @@
         out_ref[at * rows : (at + batch) * rows, :] = found.astype(jnp.bfloat16)
 
 
-def own_terms(origins, me, slots, grad_rows, near, far):
+def own_terms(origins, core, slots, grad_rows, near, far):
     width, key_width = near.shape[1], grad_rows.shape[1]
     whole = pl.BlockSpec(memory_space=pltpu.VMEM)
     return pl.pallas_call(
@@ -444,7 +457,7 @@
             transcendentals=0,
         ),
         name="own_terms",
-    )(me, slots, grad_rows, near, far)
+    )(core, slots, grad_rows, near, far)
 
 
 def bit_groups(size):
@@ -461,9 +474,24 @@
     return lax.ppermute(values, axis_name, [(i, i ^ distance) for i in range(size)])
 
 
+def stage_groups(wides, bit, values):
+    mask = (values - 1) << bit
+    return [[i | (step << bit) for step in range(values)] for i in range(wides) if not i & mask]
+
+
+def swap_blocks(rows, wides, bit, values):
+    return lax.all_to_all(
+        rows,
+        "wide",
+        split_axis=0,
+        concat_axis=0,
+        axis_index_groups=stage_groups(wides, bit, values),
+        tiled=True,
+    )
+
+
 def gather_stage(rows, wides, bit, values):
-    found = [exchange(rows, "wide", wides, step << bit) for step in range(1, values)]
-    return jnp.concatenate([rows] + found, axis=0)
+    return swap_blocks(jnp.concatenate([rows] * values, axis=0), wides, bit, values)
 
 
 def after(values, *others):
@@ -480,12 +508,8 @@
 def sum_blocks(keep, send, wides):
     total = keep.astype(jnp.float32) + exchange(send, "section", 2, 1).astype(jnp.float32)
     for bit, values in bit_groups(wides):
-        parts = total.astype(jnp.bfloat16).reshape((values, -1) + keep.shape[1:])
-        found = [
-            exchange(parts[step], "wide", wides, step << bit).astype(jnp.float32)
-            for step in range(1, values)
-        ]
-        total = sum(found, parts[0].astype(jnp.float32))
+        parts = swap_blocks(total.astype(jnp.bfloat16), wides, bit, values)
+        total = jnp.sum(parts.astype(jnp.float32).reshape((values, -1) + keep.shape[1:]), axis=0)
     return total
 
 
@@ -505,7 +529,7 @@
 ):
     wides = lax.axis_size("wide")
     devices = lax.axis_size("section") * wides
-    me = lax.axis_index("section") * wides + lax.axis_index("wide")
+    core = lax.axis_index("section") * wides
     cand_count = frames.shape[0]
     requests = req_local.shape[0]
     users, events, _ = history.shape
@@ -516,7 +540,7 @@
     ).astype(jnp.float32)
     inv_count = lax.rsqrt(jnp.sum(usable, axis=1))
     usable = usable.reshape(users, 1, events)
-    slots = slot_of(req_owner[:, 0] ^ me, wides) * cand_count + req_local
+    slots = slot_of(req_owner[:, 0] ^ core, wides) * cand_count + req_local
     stages = list(reversed(bit_groups(wides)))
     near_embedded = embedded
     for bit, values in stages:
@@ -543,7 +567,7 @@
     for distance in range(devices):
         origins[slot_of(distance, wides)] = distance
     keep, send = own_terms(
-        origins, me.reshape(1), slots.reshape(1, requests), grad_rows, near_pooled, far_pooled
+        origins, core.reshape(1), slots.reshape(1, requests), grad_rows, near_pooled, far_pooled
     )
     grad_proj = sum_blocks(keep, send, wides)
     return (logits.reshape(requests), grad_proj)

time: 113 us -> 134 us (1.19)
  blocking collectives: 0 us -> 24.8 us
  waiting for transfers between devices: 26.1 us -> 13.5 us
  local copies, waits for them, and re-layouts: 4.75 us -> 15.5 us
  starting transfers between devices: 25.9 us -> 17.4 us
  other arithmetic: 2.71 us -> 6.14 us
  Pallas kernels: 51.9 us -> 54.7 us
    ppermute x21 -> x3, starting transfers between devices: 25.9 us -> 0.58 us  [exchange(): lax.ppermute(values, axis_name, [(i, i ^ distance) for i in range(size)])]
    all_to_all x0 -> x2, blocking collectives: none -> 24.8 us  [swap_blocks(): lax.all_to_all(rows, 'wide', split_axis=0, concat_axis=0, axis_index_grou...]
    ppermute x21 -> x3, waiting for transfers between devices: 26.1 us -> 1.59 us  [exchange(): lax.ppermute(values, axis_name, [(i, i ^ distance) for i in range(size)])]
    all_to_all x0 -> x4, starting transfers between devices: none -> 16.8 us  [swap_blocks(): lax.all_to_all(rows, 'wide', split_axis=0, concat_axis=0, axis_index_grou...]
    all_to_all x0 -> x4, waiting for transfers between devices: none -> 11.9 us  [swap_blocks(): lax.all_to_all(rows, 'wide', split_axis=0, concat_axis=0, axis_index_grou...]
    unnamed x28 -> x38, local copies, waits for them, and re-layouts: 4.33 us -> 13.2 us
    pallas_call x1, Pallas kernels: 8.42 us -> 11.6 us  [attend(): pl.pallas_call(attend_kernel, grid=(users,), in_specs=[pl.BlockSpec(memor...]
    concatenate x1 -> x4, other arithmetic: 0.86 us -> 3.62 us  [gather_stage(): jnp.concatenate([rows] * values, axis=0)]
  transfers between devices with their start and end apart: 21 -> 7, of which waited for: 14 -> 4; matrix products, arithmetic and copies ran while one was open for 3% -> 3% of each run, Pallas kernels for 12% -> 19%
where the time goes in v1:
time: 134 us; the launch traced here: 133 us
  Pallas kernels  54.7 us (41%)
  blocking collectives  24.8 us (19%)
  starting transfers between devices  17.4 us (13%)
  local copies, waits for them, and re-layouts  15.5 us (12%)
  waiting for transfers between devices  13.5 us (10%)
  other arithmetic  6.14 us (5%)
    pallas_call x1, Pallas kernels, encode_block(): pl.pallas_call(functools.partial(encode_kernel, tokens), grid=(cand_count...  26.2 us
    all_to_all x2, blocking collectives, swap_blocks(): lax.all_to_all(rows, 'wide', split_axis=0, concat_axis=0, axis_index_grou...  24.8 us
    all_to_all x4, starting transfers between devices, swap_blocks(): lax.all_to_all(rows, 'wide', split_axis=0, concat_axis=0, axis_index_grou...  16.8 us
    unnamed x38, local copies, waits for them, and re-layouts  13.2 us
    all_to_all x4, waiting for transfers between devices, swap_blocks(): lax.all_to_all(rows, 'wide', split_axis=0, concat_axis=0, axis_index_grou...  11.9 us
    pallas_call x1, Pallas kernels, attend(): pl.pallas_call(attend_kernel, grid=(users,), in_specs=[pl.BlockSpec(memor...  11.6 us
    pallas_call x1, Pallas kernels, score(): pl.pallas_call(score_kernel, grid=(steps,), in_specs=[pl.BlockSpec(memory...  7.46 us
    pallas_call x1, Pallas kernels, attend_back(): pl.pallas_call(attend_back_kernel, grid=(users,), in_specs=[block, block,...  5.93 us
  transfers between devices with their start and end apart: 7, of which 4 were waited for; matrix products, arithmetic and copies ran while one was open for 3% of the time, Pallas kernels for 19%

profile of v1, /device:TPU:0, one launch (start us, length us, event | category | flops | bytes accessed | tf_op | source)
XLA Modules:
  0.0 132.9 jit_solution(5447304736600499229)
XLA Ops:
  0.6 26.2 %encode.1 = (bf16[32,1024]{1,0:T(8,128)(2,1)}, bf16[32,512]{1,0:T(8,128)(2,1)}) custom-call(bf16[1536,1024]{1,0:T(8,128)(2,1)} %bitcast.18, bf16[1536,1024]{1,0:T(8,128)(2,1)} %bitcast.19, bf16[1024,3072]{1,0:T(8,128)(2,1)} %qkv_hbm.1, bf16[1024,1024]{1,0:T(8,128)(2,1)} %out_hbm.1, bf16[1024,512]{1,0:T(8,128)(2,1)} %proj_hbm.1), custom_call_target="tpu_custom_call" | custom-call | flops 8053063680 | bytes 16777216 | tf_op jit(solution)/shard_map/encode/pallas_call | solution.py:200
  26.9 0.9 pad_maximum_fusion.3
  27.8 12.2 %all_to_all.61 = bf16[4,32,512]{2,1,0:T(8,128)(2,1)S(1)} all-to-all(bf16[4,32,512]{2,1,0:T(8,128)(2,1)S(1)} %bitcast.15), channel_id=1, replica_groups={{0,4,8,12},{1,5,9,13},{2,6,10,14},{3,7,11,15},{16,20,24,28},{17,21,25,2..., dimensions={0} | all-to-all | bytes 262144 | tf_op jit(solution)/shard_map/all_to_all | solution.py:483
  40.9 3.7 %all-to-all-start.1 = ((bf16[4,128,512]{2,1,0:T(8,128)(2,1)}), bf16[4,128,512]{2,1,0:T(8,128)(2,1)S(1)}, u32[]{:S(2)}, u32[]{:S(2)}) async-start(bf16[4,128,512]{2,1,0:T(8,128)(2,1)} %bitcast.3), calls=%async_computation.1 | async-start | bytes 1048576 | tf_op jit(solution)/shard_map/all_to_all | solution.py:483
  44.6 6.6 %all-to-all-done.1 = bf16[4,128,512]{2,1,0:T(8,128)(2,1)S(1)} async-done(((bf16[4,128,512]{2,1,0:T(8,128)(2,1)}), bf16[4,128,512]{2,1,0:T(8,128)(2,1)S(1)}, u32[]{:S(2)}, u32[]{:S(2)}) %all-to-all-start.1) | async-done | bytes 524320 | tf_op jit(solution)/shard_map/all_to_all | solution.py:483
  52.2 3.5 %all-to-all-start.2 = ((bf16[4,32,1024]{2,1,0:T(8,128)(2,1)}), bf16[4,32,1024]{2,1,0:T(8,128)(2,1)S(1)}, u32[]{:S(2)}, u32[]{:S(2)}) async-start(bf16[4,32,1024]{2,1,0:T(8,128)(2,1)} %bitcast.6), calls=%async_computation.2 | async-start | bytes 524288 | tf_op jit(solution)/shard_map/all_to_all | solution.py:483
  55.7 0.9 reshape.60.slots_ref
  58.6 11.6 %attend.1 = (bf16[768,512]{1,0:T(8,128)(2,1)}, f32[768,512]{1,0:T(8,128)}, bf16[768,2048]{1,0:T(8,128)(2,1)}) custom-call(f32[4]{0:T(128)} %rsqrt.3.inv_ref, s32[768,1]{1,0:T(8,128)} %reshape.60.slots_ref, bf16[512,512]{1,0:T(8,128)(2,1)} %bitcast.17, bf16[512,512]{1,0:T(8,128)(2,1)} %copy-done.18, bf16[4,2048,512]{2,1,0:T(8,128)(2,1)} %history_ref.3, ...), custom_call_target="tpu_custom_call" | custom-call | flops 3221225472 | bytes 16777216 | tf_op jit(solution)/shard_map/attend/pallas_call | solution.py:270
  70.2 1.1 pad_maximum_fusion
  71.3 4.4 %all-to-all-start.3 = ((bf16[4,128,1024]{2,1,0:T(8,128)(2,1)}), bf16[4,128,1024]{2,1,0:T(8,128)(2,1)}, u32[]{:S(2)}, u32[]{:S(2)}) async-start(bf16[4,128,1024]{2,1,0:T(8,128)(2,1)} %bitcast.8), calls=%async_computation.3 | async-start | bytes 2097152 | tf_op jit(solution)/shard_map/all_to_all | solution.py:483
  76.0 1.9 %copy-done.6 = bf16[1536,1024]{1,0:T(8,128)(2,1)S(1)} copy-done((bf16[1536,1024]{1,0:T(8,128)(2,1)S(1)}, bf16[1536,1024]{1,0:T(8,128)(2,1)}, u32[]{:S(2)}) %copy-start.6) | copy-done | bytes 3145752
  77.9 1.4 %copy-done.8 = f32[768,512]{1,0:T(8,128)S(1)} copy-done((f32[768,512]{1,0:T(8,128)S(1)}, f32[768,512]{1,0:T(8,128)}, u32[]{:S(2)}) %copy-start.8) | copy-done | bytes 1572888
  79.3 1.1 copy-done.9
  80.4 7.5 %score.1 = (f32[768,1]{1,0:T(8,128)S(1)}, bf16[768,512]{1,0:T(8,128)(2,1)S(1)}, f32[768,512]{1,0:T(8,128)S(1)}) custom-call(f32[4]{0:T(128)S(1)} %copy-done.7, bf16[768,512]{1,0:T(8,128)(2,1)S(1)} %copy-done.9, f32[768,512]{1,0:T(8,128)S(1)} %copy-done.8, s32[768,1]{1,0:T(8,128)S(1)} %reshape.61.labels_ref, bf16[1536,1024]{1,0:T(8,128)(2,1)S(1)} %copy-done.6, ...), custom_call_target="tpu_custom_call" | custom-call | flops 4831838208 | bytes 8388608 | tf_op jit(solution)/shard_map/score/pallas_call | solution.py:346
  87.9 1.1 copy-done.2
  90.3 3.4 %copy-done = bf16[4,2048,512]{2,1,0:T(8,128)(2,1)S(1)} copy-done((bf16[4,2048,512]{2,1,0:T(8,128)(2,1)S(1)}, bf16[4,2048,512]{2,1,0:T(8,128)(2,1)}, u32[]{:S(2)}) %copy-start) | copy-done | bytes 8388632
  93.7 1.4 %copy-done.3 = f32[768,512]{1,0:T(8,128)S(1)} copy-done((f32[768,512]{1,0:T(8,128)S(1)}, f32[768,512]{1,0:T(8,128)}, u32[]{:S(2)}) %copy-start.3) | copy-done | bytes 1572888
  95.1 1.1 copy-done.5
  96.3 5.9 %attend_back.1.grad_rows_ref = bf16[768,512]{1,0:T(8,128)(2,1)S(1)} custom-call(bf16[768,512]{1,0:T(8,128)(2,1)S(1)} %copy-done.5, f32[768,512]{1,0:T(8,128)S(1)} %copy-done.3, bf16[768,2048]{1,0:T(8,128)(2,1)S(1)} %copy-done.1, bf16[4,2048,512]{2,1,0:T(8,128)(2,1)S(1)} %copy-done), custom_call_target="tpu_custom_call" | custom-call | flops 3221225472 | bytes 16777216 | tf_op jit(solution)/shard_map/attend_back/pallas_call | solution.py:393
  102.2 3.5 %own_terms.1 = (bf16[512,512]{1,0:T(8,128)(2,1)S(1)}, bf16[512,512]{1,0:T(8,128)(2,1)S(1)}) custom-call(s32[1]{0:T(128)} %bitcast.5.core_ref, s32[1,768]{1,0:T(1,128)S(1)} %reshape.59.slots_ref, bf16[768,512]{1,0:T(8,128)(2,1)S(1)} %attend_back.1.grad_rows_ref, bf16[512,1024]{1,0:T(8,128)(2,1)} %bitcast.9.near_ref, ...), custom_call_target="tpu_custom_call" | custom-call | flops 1879048192 | bytes 8388608 | tf_op jit(solution)/shard_map/own_terms/pallas_call | solution.py:447
  106.2 1.6 %collective-permute-done.2 = bf16[512,512]{1,0:T(8,128)(2,1)S(1)} collective-permute-done((bf16[512,512]{1,0:T(8,128)(2,1)S(1)}, bf16[512,512]{1,0:T(8,128)(2,1)S(1)}, u32[]{:S(2)}, u32[]{:S(2)}) %collective-permute-start.2) | collective-permute-done | bytes 524320 | tf_op jit(solution)/shard_map/ppermute | solution.py:474
  107.9 12.6 %all_to_all.62 = bf16[4,128,512]{2,1,0:T(8,128)(2,1)S(1)} all-to-all(bf16[4,128,512]{2,1,0:T(8,128)(2,1)S(1)} %bitcast.12), channel_id=1, replica_groups={{0,1,2,3},{4,5,6,7},{8,9,10,11},{12,13,14,15},{16,17,18,19},{20,21,22,2..., dimensions={0} | all-to-all | bytes 1048576 | tf_op jit(solution)/shard_map/all_to_all | solution.py:483
  121.2 5.1 %all-to-all-start.5 = ((bf16[4,32,512]{2,1,0:T(8,128)(2,1)}), bf16[4,32,512]{2,1,0:T(8,128)(2,1)S(1)}, u32[]{:S(2)}, u32[]{:S(2)}) async-start(bf16[4,32,512]{2,1,0:T(8,128)(2,1)} %bitcast.11), calls=%async_computation.5 | async-start | bytes 262144 | tf_op jit(solution)/shard_map/all_to_all | solution.py:483
  127.1 5.2 %all-to-all-done.5 = bf16[4,32,512]{2,1,0:T(8,128)(2,1)S(1)} async-done(((bf16[4,32,512]{2,1,0:T(8,128)(2,1)}), bf16[4,32,512]{2,1,0:T(8,128)(2,1)S(1)}, u32[]{:S(2)}, u32[]{:S(2)}) %all-to-all-start.5) | async-done | bytes 131104 | tf_op jit(solution)/shard_map/all_to_all | solution.py:483
  (53 shorter events, 7.9 us)
Async XLA Ops:
  26.8 17.8 %copy-start.15 = (s32[768,1]{0,1:T(1,128)S(1)}, s32[768,1]{0,1:T(1,128)}, u32[]{:S(2)}) copy-start(s32[768,1]{0,1:T(1,128)} %param.21) | copy-start | bytes 9220
  26.9 24.4 %copy-start.12 = (s32[4,2048]{1,0:T(4,128)S(1)}, s32[4,2048]{1,0:T(4,128)}, u32[]{:S(2)}) copy-start(s32[4,2048]{1,0:T(4,128)} %param.20) | copy-start | bytes 98308
  26.9 24.4 %copy-start.17 = (s32[4]{0:T(128)S(1)}, s32[4]{0:T(128)}, u32[]{:S(2)}) copy-start(s32[4]{0:T(128)} %param.19) | copy-start | bytes 52
  26.9 24.6 %copy-start.11 = (bf16[32,1024]{1,0:T(8,128)(2,1)S(1)}, bf16[32,1024]{1,0:T(8,128)(2,1)}, u32[]{:S(2)}) copy-start(bf16[32,1024]{1,0:T(8,128)(2,1)} %get-tuple-element.23) | copy-start | bytes 196612
  26.9 28.8 %copy-start.14 = (s32[768]{0:T(1024)S(1)}, s32[768]{0:T(1024)}, u32[]{:S(2)}) copy-start(s32[768]{0:T(1024)} %param.22) | copy-start | bytes 9220
  40.9 10.3 %all-to-all-start.1 = ((bf16[4,128,512]{2,1,0:T(8,128)(2,1)}), bf16[4,128,512]{2,1,0:T(8,128)(2,1)S(1)}, u32[]{:S(2)}, u32[]{:S(2)}) async-start(bf16[4,128,512]{2,1,0:T(8,128)(2,1)} %bitcast.3), calls=%async_computation.1 | async-start | bytes 1048576 | tf_op jit(solution)/shard_map/all_to_all | solution.py:483
  51.2 6.6 %copy-start.10 = (bf16[4,128,512]{2,1,0:T(8,128)(2,1)}, bf16[4,128,512]{2,1,0:T(8,128)(2,1)S(1)}, u32[]{:S(2)}) copy-start(bf16[4,128,512]{2,1,0:T(8,128)(2,1)S(1)} %all-to-all-done.1) | copy-start | bytes 1572868
  51.2 6.6 %collective-permute-start = (bf16[512,512]{1,0:T(8,128)(2,1)S(1)}, bf16[512,512]{1,0:T(8,128)(2,1)S(1)}, u32[]{:S(2)}, u32[]{:S(2)}) collective-permute-start(bf16[512,512]{1,0:T(8,128)(2,1)S(1)} %bitcast.16), channel_id=1, source_target_pairs={{0,16},{16,0},{1,17},{17,1},{2,18},{18,2},{3,19},{19,3},{4,20},{20... | collective-permute-start | bytes 1572872 | tf_op jit(solution)/shard_map/ppermute | solution.py:474
  52.2 18.1 %all-to-all-start.2 = ((bf16[4,32,1024]{2,1,0:T(8,128)(2,1)}), bf16[4,32,1024]{2,1,0:T(8,128)(2,1)S(1)}, u32[]{:S(2)}, u32[]{:S(2)}) async-start(bf16[4,32,1024]{2,1,0:T(8,128)(2,1)} %bitcast.6), calls=%async_computation.2 | async-start | bytes 524288 | tf_op jit(solution)/shard_map/all_to_all | solution.py:483
  70.2 5.6 %copy-start.13 = (s32[768]{0:T(1024)S(1)}, s32[768]{0:T(1024)}, u32[]{:S(2)}) copy-start(s32[768]{0:T(1024)} %param.23) | copy-start | bytes 9220
  70.2 5.8 %copy-start.16 = (bf16[1024]{0:T(1024)(128)(2,1)S(1)}, bf16[1024]{0:T(1024)(128)(2,1)}, u32[]{:S(2)}) copy-start(bf16[1024]{0:T(1024)(128)(2,1)} %param.17) | copy-start | bytes 6148
  70.2 5.8 %copy-start.7 = (f32[4]{0:T(128)S(1)}, f32[4]{0:T(128)}, u32[]{:S(2)}) copy-start(f32[4]{0:T(128)} %rsqrt.3.inv_ref) | copy-start | bytes 52
  71.3 18.8 %all-to-all-start.3 = ((bf16[4,128,1024]{2,1,0:T(8,128)(2,1)}), bf16[4,128,1024]{2,1,0:T(8,128)(2,1)}, u32[]{:S(2)}, u32[]{:S(2)}) async-start(bf16[4,128,1024]{2,1,0:T(8,128)(2,1)} %bitcast.8), calls=%async_computation.3 | async-start | bytes 2097152 | tf_op jit(solution)/shard_map/all_to_all | solution.py:483
  76.0 1.9 %copy-start.6 = (bf16[1536,1024]{1,0:T(8,128)(2,1)S(1)}, bf16[1536,1024]{1,0:T(8,128)(2,1)}, u32[]{:S(2)}) copy-start(bf16[1536,1024]{1,0:T(8,128)(2,1)} %mlp_ref.1) | copy-start | bytes 9437188
  77.9 1.4 %copy-start.8 = (f32[768,512]{1,0:T(8,128)S(1)}, f32[768,512]{1,0:T(8,128)}, u32[]{:S(2)}) copy-start(f32[768,512]{1,0:T(8,128)} %get-tuple-element.17.attended_ref) | copy-start | bytes 4718596
  79.3 1.1 copy-start.9
  80.4 9.9 %copy-start.1 = (bf16[768,2048]{1,0:T(8,128)(2,1)S(1)}, bf16[768,2048]{1,0:T(8,128)(2,1)}, u32[]{:S(2)}) copy-start(bf16[768,2048]{1,0:T(8,128)(2,1)} %get-tuple-element.21.slope_ref) | copy-start | bytes 9437188
  87.9 1.2 copy-start.2
  90.1 12.1 %collective-permute-start.1 = (bf16[512,1024]{1,0:T(8,128)(2,1)}, bf16[512,1024]{1,0:T(8,128)(2,1)S(1)}, u32[]{:S(2)}, u32[]{:S(2)}) collective-permute-start(bf16[512,1024]{1,0:T(8,128)(2,1)} %bitcast.9.near_ref), channel_id=1, source_target_pairs={{0,16},{16,0},{1,17},{17,1},{2,18},{18,2},{3,19},{19,3},{4,20},{20... | collective-permute-start | bytes 3145736 | tf_op jit(solution)/shard_map/ppermute | solution.py:474
  90.3 3.4 %copy-start = (bf16[4,2048,512]{2,1,0:T(8,128)(2,1)S(1)}, bf16[4,2048,512]{2,1,0:T(8,128)(2,1)}, u32[]{:S(2)}) copy-start(bf16[4,2048,512]{2,1,0:T(8,128)(2,1)} %history_ref.3) | copy-start | bytes 25165828
  93.7 1.4 %copy-start.3 = (f32[768,512]{1,0:T(8,128)S(1)}, f32[768,512]{1,0:T(8,128)}, u32[]{:S(2)}) copy-start(f32[768,512]{1,0:T(8,128)} %copy-done.2) | copy-start | bytes 4718596
  95.1 1.1 copy-start.5
  105.8 2.0 %collective-permute-start.2 = (bf16[512,512]{1,0:T(8,128)(2,1)S(1)}, bf16[512,512]{1,0:T(8,128)(2,1)S(1)}, u32[]{:S(2)}, u32[]{:S(2)}) collective-permute-start(bf16[512,512]{1,0:T(8,128)(2,1)S(1)} %get-tuple-element.27), channel_id=1, source_target_pairs={{0,16},{16,0},{1,17},{17,1},{2,18},{18,2},{3,19},{19,3},{4,20},{20... | collective-permute-start | bytes 1572872 | tf_op jit(solution)/shard_map/ppermute | solution.py:474
  121.2 11.0 %all-to-all-start.5 = ((bf16[4,32,512]{2,1,0:T(8,128)(2,1)}), bf16[4,32,512]{2,1,0:T(8,128)(2,1)S(1)}, u32[]{:S(2)}, u32[]{:S(2)}) async-start(bf16[4,32,512]{2,1,0:T(8,128)(2,1)} %bitcast.11), calls=%async_computation.5 | async-start | bytes 262144 | tf_op jit(solution)/shard_map/all_to_all | solution.py:483
  (2 other events, 1.7 us)
